TPU v7x, 256 devices: a whole 4x4x8 slice. The times are simulated.
256 devices in a mesh: circ: 128 (over x_lo, z, y, core), mode: 2 (over x_hi).
Axes of the slice: x: 4 (x_hi: 2, x_lo: 2; x = x_hi * 2 + x_lo), y: 4, z: 8, core: 2. Of those that a mesh axis runs over, the one named last changes fastest.
Arguments:
- right_side: float32 [20, 3, 256, 1024], P('mode', None, 'circ'), may hold values from -5 to 5
- stiffness: float32 [4, 256, 1024], P(None, 'circ'), may hold values from -0.15 to 2, as said below
- pairing: int32 [3, 20], replicated, may hold values from 0 to 19, each once within a row
- coupling: float32 [3, 20], replicated, may hold values from -1 to 1
Outputs:
- solution_field: float32 [20, 3, 256, 1024], P('mode', None, 'circ')
- residual: float32 [20, 3, 256, 1024], P('mode', None, 'circ')
Inputs may be any that keep to these rules, and one draw needn't show every extreme that they name: `pairing`: each row is a permutation of the 20 chaos modes. The mean stiffness lies in [1, 2], the three random modes in [-0.15, 0.15].
All inputs are finite; a program needn't handle non-finite values.
Results may differ from a plain program's by a relative error of at most 0.001.
Values sent between devices are 32-bit elements; how exact they have to be, the bound alone decides.
A program may use at most 64 MiB of HBM per device.

v0:
```python
import math

import jax
import jax.numpy as jnp
from jax import lax
from jax.sharding import PartitionSpec as P

KM = 4
NL = 16
NT = 64
ITERS = 2


LAME_RATIO = 1.0


def padded_2(cells, sides, width):
    for axis, dim in sides:
        count = lax.axis_size(axis)
        head = lax.slice_in_dim(cells, 0, width, axis=dim)
        tail = lax.slice_in_dim(cells, cells.shape[dim] - width, cells.shape[dim], axis=dim)
        cells = jnp.concatenate(
            [
                lax.ppermute(tail, axis, [(i, (i + 1) % count) for i in range(count)]),
                cells,
                lax.ppermute(head, axis, [((i + 1) % count, i) for i in range(count)]),
            ],
            axis=dim,
        )
    return cells


def dir_weight(component, direction):
    return 1.0 + LAME_RATIO if component == direction else 1.0


def weight_column(direction, trailing):
    values = jnp.array([dir_weight(comp_no, direction) for comp_no in range(3)], jnp.float32)
    return values.reshape((3,) + (1,) * trailing)


def stencil(padded, coeff_pad, n_long, n_trans):
    num_modes, num_comps, span_pad, num_cells = padded.shape
    span = span_pad - 2
    center = padded[:, :, 1:-1]
    coeff_mid = coeff_pad[1:-1]
    right_face = 0.5 * (coeff_mid + coeff_pad[2:])
    left_face = 0.5 * (coeff_mid + coeff_pad[:-2])
    circ_part = right_face * (center - padded[:, :, 2:]) + left_face * (center - padded[:, :, :-2])
    field = center.reshape(num_modes, num_comps, span, n_long, n_trans)
    coeff_cube = coeff_mid.reshape(span, n_long, n_trans)
    long_face = 0.5 * (coeff_cube[:, :-1] + coeff_cube[:, 1:])
    long_flux = long_face * (field[:, :, :, 1:] - field[:, :, :, :-1])
    zero_row = jnp.zeros((num_modes, num_comps, span, 1, n_trans), jnp.float32)
    long_part = jnp.concatenate([zero_row, long_flux], 3) - jnp.concatenate(
        [long_flux, zero_row], 3
    )
    edge_pad = jnp.pad(coeff_cube, ((0, 0), (0, 0), (1, 1)), mode="edge")
    trans_face = 0.5 * (edge_pad[:, :, :-1] + edge_pad[:, :, 1:])
    zero_pad = jnp.pad(field, ((0, 0), (0, 0), (0, 0), (0, 0), (1, 1)))
    trans_flux = trans_face * (zero_pad[..., 1:] - zero_pad[..., :-1])
    trans_part = trans_flux[..., :-1] - trans_flux[..., 1:]
    inner = weight_column(1, 3) * long_part + weight_column(2, 3) * trans_part
    return weight_column(0, 2) * circ_part + inner.reshape(num_modes, num_comps, span, num_cells)


def build_coupling(pairing, coupling):
    modes = pairing.shape[1]
    onehot = (pairing[:, :, None] == jnp.arange(modes, dtype=jnp.int32)[None, None, :]).astype(
        jnp.float32
    )
    halfway = coupling[:, :, None] * onehot
    return 0.5 * (halfway + jnp.swapaxes(halfway, 1, 2))


def hartley_table(size):
    indices = jnp.arange(size, dtype=jnp.int32)
    product = indices[:, None] * indices[None, :] % size
    angle = 2.0 * math.pi / size * product.astype(jnp.float32)
    return jnp.cos(angle) + jnp.sin(angle)


def cosine_table(size):
    indices = jnp.arange(size, dtype=jnp.int32)
    product = (2 * indices[:, None] + 1) * indices[None, :] % (4 * size)
    return jnp.cos(math.pi / (2 * size) * product.astype(jnp.float32))


def sine_table(size):
    indices = jnp.arange(size, dtype=jnp.int32) + 1
    product = indices[:, None] * indices[None, :] % (2 * (size + 1))
    return jnp.sin(math.pi / (size + 1) * product.astype(jnp.float32))


def eigen_denominator(freq_circ, freq_long, freq_trans, n_circ, n_long, n_trans):
    lam_circ = 2.0 - 2.0 * jnp.cos(2.0 * math.pi / n_circ * freq_circ.astype(jnp.float32))
    lam_long = 2.0 - 2.0 * jnp.cos(math.pi / n_long * freq_long.astype(jnp.float32))
    lam_trans = 2.0 - 2.0 * jnp.cos(math.pi / (n_trans + 1) * (freq_trans + 1).astype(jnp.float32))
    norm_long = jnp.where(freq_long == 0, 1.0 * n_long, 0.5 * n_long).astype(jnp.float32)
    scale = n_circ * norm_long * (0.5 * (n_trans + 1))
    rows = []
    for comp_no in range(3):
        lam = (
            dir_weight(comp_no, 0) * lam_circ
            + dir_weight(comp_no, 1) * lam_long
            + dir_weight(comp_no, 2) * lam_trans
        )
        rows.append(lam * scale)
    return jnp.stack(rows, 0)


def on_device(right_side, stiffness, pairing, coupling):
    highest = lax.Precision.HIGHEST
    local_modes, num_comps, local_circ, num_cells = right_side.shape
    circ_devices = lax.axis_size("circ")
    full_circ = local_circ * circ_devices
    local_cols = num_cells // circ_devices
    gmat = build_coupling(pairing, coupling)
    coeff_pad = padded_2(stiffness, (("circ", 1),), 1)
    row_start = lax.axis_index("mode") * local_modes
    htab = hartley_table(full_circ)
    ctab = cosine_table(NL)
    stab = sine_table(NT)
    column_ids = lax.axis_index("circ") * local_cols + jnp.arange(local_cols, dtype=jnp.int32)
    denom = eigen_denominator(
        jnp.arange(full_circ, dtype=jnp.int32)[None, :],
        (column_ids // NT)[:, None],
        (column_ids % NT)[:, None],
        full_circ,
        NL,
        NT,
    )

    def spectral(piece):
        lanes = jnp.swapaxes(piece, 2, 3)
        scaled = jnp.einsum("pcqn,nk->pcqk", lanes, htab, precision=highest) / denom[None]
        restored = jnp.einsum("pcqk,kn->pcqn", scaled, htab, precision=highest)
        return lax.all_to_all(
            jnp.swapaxes(restored, 2, 3), "circ", split_axis=2, concat_axis=3, tiled=True
        )

    def precondition(values):
        field = values.reshape(local_modes, num_comps, local_circ, NL, NT)
        spec = jnp.einsum("pcnlt,lm->pcnmt", field, ctab, precision=highest)
        spec = jnp.einsum("pcnmt,ts->pcnms", spec, stab, precision=highest)
        spec = spec.reshape(local_modes, num_comps, local_circ, num_cells)
        spec = spectral(lax.all_to_all(spec, "circ", split_axis=3, concat_axis=2, tiled=True))
        spec = spec.reshape(local_modes, num_comps, local_circ, NL, NT)
        spec = jnp.einsum("pcnms,lm->pcnls", spec, ctab, precision=highest)
        spec = jnp.einsum("pcnls,ts->pcnlt", spec, stab, precision=highest)
        return spec.reshape(local_modes, num_comps, local_circ, num_cells)

    def precond_sum(residual, smoothed):
        return lax.psum(jnp.sum(residual * smoothed), ("circ", "mode"))

    solution_field = jnp.zeros_like(right_side)
    residual = right_side
    smoothed = precondition(residual)
    direction = smoothed
    inner_now = precond_sum(residual, smoothed)
    for iteration in range(ITERS):
        padded = padded_2(direction, (("circ", 2),), 1)
        result = stencil(padded, coeff_pad[0], NL, NT)
        empty = jnp.zeros((local_modes, num_comps, local_circ, num_cells), jnp.float32)
        total = empty
        fold_piece = lax.all_gather(padded, "mode", axis=0, tiled=True)
        piece_modes = fold_piece.shape[0]
        for order in range(1, KM):
            term = stencil(fold_piece, coeff_pad[order], NL, NT)
            block = lax.dynamic_slice(gmat[order - 1], (row_start, 0), (local_modes, piece_modes))
            total = total + jnp.einsum("ij,jcnq->icnq", block, term, precision=highest)
        image = result + total
        alpha = inner_now / lax.psum(jnp.sum(direction * image), ("circ", "mode"))
        solution_field = solution_field + alpha * direction
        residual = residual - alpha * image
        if iteration + 1 < ITERS:
            smoothed = precondition(residual)
            inner_next = precond_sum(residual, smoothed)
            direction = smoothed + inner_next / inner_now * direction
            inner_now = inner_next
    return (solution_field, residual)


def solution(mesh):
    placed = (P("mode", None, "circ", None), P(None, "circ", None), P(), P())
    return jax.shard_map(
        on_device,
        mesh=mesh,
        in_specs=placed,
        out_specs=(P("mode", None, "circ", None), P("mode", None, "circ", None)),
        check_vma=False,
    )
```

profile of v0, /device:TPU:1, one launch (start us, length us, event | category | flops | bytes accessed | tf_op | source)
XLA Modules:
  0.0 514.9 jit_solution(15589782013960005664)
XLA Ops:
  2.6 1.5 fusion.67
  4.2 4.2 copy.171
  8.3 7.0 %reshape.631 = f32[128,1,480]{2,1,0:T(1,128)} reshape(f32[1024,3,2,10]{3,2,1,0:T(2,128)S(1)} %bitcast.154) | data formatting | bytes 491520
  15.4 14.9 %all-to-all-start = ((f32[128,1,480]{2,1,0:T(1,128)}), f32[128,1,480]{2,1,0:T(1,128)S(1)}, u32[]{:S(2)}, u32[]{:S(2)}) async-start(f32[128,1,480]{2,1,0:T(1,128)} %reshape.631), calls=%async_computation | async-start | bytes 524288 | tf_op jit(solution)/shard_map/all_to_all | solution.py:147
  37.1 8.2 %all-to-all-done = f32[128,1,480]{2,1,0:T(1,128)S(1)} async-done(((f32[128,1,480]{2,1,0:T(1,128)}), f32[128,1,480]{2,1,0:T(1,128)S(1)}, u32[]{:S(2)}, u32[]{:S(2)}) %all-to-all-start) | async-done | bytes 245792 | tf_op jit(solution)/shard_map/all_to_all | solution.py:147
  46.0 2.1 reduce
  48.0 5.4 %reshape.632 = f32[1024,3,2,10]{3,2,1,0:T(2,128)S(1)} reshape(f32[128,480]{1,0:T(8,128)} %reduce) | data formatting | bytes 491520
  53.4 1.9 copy.173
  55.3 2.4 copy.124
  59.1 2.5 convolution_bitcast_fusion.5
  61.6 2.0 copy.125
  63.6 4.4 reshape.633
  68.0 6.7 %all-to-all-start.1 = ((f32[128,1,480]{2,1,0:T(1,128)}), f32[128,1,480]{2,1,0:T(1,128)S(1)}, u32[]{:S(2)}, u32[]{:S(2)}) async-start(f32[128,1,480]{2,1,0:T(1,128)} %reshape.633), calls=%async_computation.1 | async-start | bytes 524288 | tf_op jit(solution)/shard_map/all_to_all | solution.py:138
  76.7 13.2 %all-to-all-done.1 = f32[128,1,480]{2,1,0:T(1,128)S(1)} async-done(((f32[128,1,480]{2,1,0:T(1,128)}), f32[128,1,480]{2,1,0:T(1,128)S(1)}, u32[]{:S(2)}, u32[]{:S(2)}) %all-to-all-start.1) | async-done | bytes 245792 | tf_op jit(solution)/shard_map/all_to_all | solution.py:138
  89.9 2.1 reduce.1
  91.9 2.6 reshape.634
  94.6 6.5 %copy.127 = f32[10,3,2,128,8]{4,3,2,1,0:T(8,128)} copy(f32[10,3,2,128,8]{0,4,1,2,3:T(8,128)S(1)} %bitcast.158) | data formatting | bytes 491520 | tf_op jit(solution)/shard_map/all_to_all | solution.py:138
  101.1 3.1 reshape.603
  109.4 2.4 collective-permute-done.1
  112.7 10.8 %all_gather.6 = f32[20,3,4,1024]{3,2,1,0:T(4,128)S(1)} all-gather(f32[10,3,4,1024]{3,2,1,0:T(4,128)S(1)} %pad_maximum_fusion.1), channel_id=1, replica_groups=mesh['circ'=128,'mode'=2] {'mode'}, dimensions={0}, use_global_device_ids=true | all-gather | bytes 1474560 | tf_op jit(solution)/shard_map/all_gather | solution.py:166
  124.6 1.6 reshape.608
  128.3 2.5 fusion.9
  130.8 2.5 reshape.609
  133.3 2.5 reshape.611
  137.1 2.8 multiply_add_fusion.4
  142.7 81.1 %all-reduce.20 = (f32[]{:T(128)}, f32[]{:T(128)}) all-reduce(f32[]{:T(128)} %multiply_reduce_fusion.2, f32[]{:T(128)} %get-tuple-element.68), channel_id=1, replica_groups=mesh['circ'=128,'mode'=2] {'circ','mode'}, use_global_device_ids=true, to_apply=%region_1.2 | all-reduce | flops 2 | bytes 16 | tf_op jit(solution)/shard_map/psum | solution.py:154
  227.2 3.5 copy.176
  230.8 6.5 %reshape.635 = f32[128,1,480]{2,1,0:T(1,128)S(1)} reshape(f32[1024,3,2,10]{3,2,1,0:T(2,128)} %bitcast.159) | data formatting | bytes 491520
  237.2 22.0 %all_to_all.66 = f32[128,1,480]{2,1,0:T(1,128)S(1)} all-to-all(f32[128,1,480]{2,1,0:T(1,128)S(1)} %reshape.635), channel_id=1, replica_groups=mesh['circ'=128,'mode'=2] {'circ'}, dimensions={0} | all-to-all | bytes 491520 | tf_op jit(solution)/shard_map/all_to_all | solution.py:147
  260.6 6.5 %reshape.636 = f32[1024,3,2,10]{3,2,1,0:T(2,128)} reshape(f32[128,480]{1,0:T(8,128)S(1)} %reduce.2) | data formatting | bytes 491520
  267.0 3.8 copy.178
  270.8 2.4 copy.148
  276.1 2.2 copy.149
  278.3 5.3 %reshape.637 = f32[128,1,480]{2,1,0:T(1,128)S(1)} reshape(f32[256,3,8,10]{3,2,1,0:T(8,128)} %bitcast.162) | data formatting | bytes 491520
  283.6 20.3 %all_to_all.67 = f32[128,1,480]{2,1,0:T(1,128)S(1)} all-to-all(f32[128,1,480]{2,1,0:T(1,128)S(1)} %reshape.637), channel_id=1, replica_groups=mesh['circ'=128,'mode'=2] {'circ'}, dimensions={0} | all-to-all | bytes 491520 | tf_op jit(solution)/shard_map/all_to_all | solution.py:138
  305.3 3.4 reshape.638
  308.7 7.5 %copy.151 = f32[10,3,2,128,8]{4,3,2,1,0:T(8,128)} copy(f32[10,3,2,128,8]{0,4,1,2,3:T(8,128)} %bitcast.163) | data formatting | bytes 491520 | tf_op jit(solution)/shard_map/all_to_all | solution.py:138
  316.2 3.1 reshape.616
  321.7 72.7 %psum.30 = f32[]{:T(128)} all-reduce(f32[]{:T(128)} %fusion.28), channel_id=1, replica_groups=mesh['circ'=128,'mode'=2] {'circ','mode'}, use_global_device_ids=true, to_apply=%region_5.6 | all-reduce | flops 1 | bytes 8 | tf_op jit(solution)/shard_map/psum | solution.py:154
  398.7 2.8 collective-permute-done.4
  401.9 10.1 %all_gather.7 = f32[20,3,4,1024]{3,2,1,0:T(4,128)S(1)} all-gather(f32[10,3,4,1024]{3,2,1,0:T(4,128)S(1)} %copy.156), channel_id=1, replica_groups=mesh['circ'=128,'mode'=2] {'mode'}, dimensions={0}, use_global_device_ids=true | all-gather | bytes 1474560 | tf_op jit(solution)/shard_map/all_gather | solution.py:166
  413.1 1.6 reshape.619
  416.3 2.5 fusion.3
  418.8 2.5 reshape.620
  421.4 2.5 reshape.621
  425.3 2.8 multiply_add_fusion
  429.4 1.5 multiply_reduce_fusion
  430.9 80.2 %psum.31 = f32[]{:T(128)} all-reduce(f32[]{:T(128)} %get-tuple-element.70), channel_id=1, replica_groups=mesh['circ'=128,'mode'=2] {'circ','mode'}, use_global_device_ids=true, to_apply=%region_7.8 | all-reduce | flops 1 | bytes 8 | tf_op jit(solution)/shard_map/psum | solution.py:173
  (203 shorter events, 46.1 us)
Async XLA Ops:
  0.6 103.6 %copy-start.41 = (s32[16]{0:T(128)}, s32[16]{0:T(128)S(1)}, u32[]{:S(2)}) copy-start(s32[16]{0:T(128)S(1)} %multiply_add_fusion.8) | copy-start | bytes 196
  0.7 104.2 %copy-start.37 = (s32[64]{0:T(128)}, s32[64]{0:T(128)S(1)}, u32[]{:S(2)}) copy-start(s32[64]{0:T(128)S(1)} %iota_add_fusion.1) | copy-start | bytes 772
  4.2 26.1 %copy-start.2 = (f32[4,2,1024]{2,1,0:T(2,128)S(1)}, f32[4,2,1024]{2,1,0:T(2,128)}, u32[]{:S(2)}) copy-start(f32[4,2,1024]{2,1,0:T(2,128)} %param.29) | copy-start | bytes 98308
  4.2 28.6 %copy-start.53 = (f32[3,20]{1,0:T(4,128)S(1)}, f32[3,20]{1,0:T(4,128)}, u32[]{:S(2)}) copy-start(f32[3,20]{1,0:T(4,128)} %param.31) | copy-start | bytes 724
  4.2 28.6 %copy-start.54 = (s32[3,20]{1,0:T(4,128)S(1)}, s32[3,20]{1,0:T(4,128)}, u32[]{:S(2)}) copy-start(s32[3,20]{1,0:T(4,128)} %param.30) | copy-start | bytes 724
  15.4 30.0 %all-to-all-start = ((f32[128,1,480]{2,1,0:T(1,128)}), f32[128,1,480]{2,1,0:T(1,128)S(1)}, u32[]{:S(2)}, u32[]{:S(2)}) async-start(f32[128,1,480]{2,1,0:T(1,128)} %reshape.631), calls=%async_computation | async-start | bytes 524288 | tf_op jit(solution)/shard_map/all_to_all | solution.py:147
  30.3 3.6 collective-permute-start
  31.3 44.2 %collective-permute-start.2 = (f32[4,1,1024]{2,1,0:T(1,128)S(1)}, f32[4,1,1024]{2,1,0:T(1,128)S(1)}, u32[]{:S(2)}, u32[]{:S(2)}) collective-permute-start(f32[4,1,1024]{2,1,0:T(1,128)S(1)} %get-tuple-element.50), channel_id=1, source_target_pairs={{0,2},{2,4},{4,6},{6,8},{8,10},{10,12},{12,14},{14,16},{16,18},{18... | collective-permute-start | bytes 49160 | tf_op jit(solution)/shard_map/ppermute | solution.py:24
  33.6 24.1 %copy-start.39 = (f32[3,8,256]{2,1,0:T(8,128)}, f32[3,8,256]{2,1,0:T(8,128)S(1)}, u32[]{:S(2)}) copy-start(f32[3,8,256]{2,1,0:T(8,128)S(1)} %pad_maximum_fusion.6) | copy-start | bytes 73732
  68.0 21.8 %all-to-all-start.1 = ((f32[128,1,480]{2,1,0:T(1,128)}), f32[128,1,480]{2,1,0:T(1,128)S(1)}, u32[]{:S(2)}, u32[]{:S(2)}) async-start(f32[128,1,480]{2,1,0:T(1,128)} %reshape.633), calls=%async_computation.1 | async-start | bytes 524288 | tf_op jit(solution)/shard_map/all_to_all | solution.py:138
  104.2 2.7 copy-start.45
  104.2 2.7 copy-start.49
  106.1 3.2 collective-permute-start.3
  106.6 5.1 collective-permute-start.1
  137.0 2.9 copy-start.35
  137.0 3.5 copy-start.33
  137.0 4.1 copy-start.1
  137.1 4.1 copy-start.8
  137.1 4.1 copy-start.21
  137.1 4.1 copy-start.26
  137.1 4.1 copy-start.31
  137.1 4.1 copy-start.43
  140.6 85.2 %copy-start.42 = (s32[16]{0:T(128)S(1)}, s32[16]{0:T(128)}, u32[]{:S(2)}) copy-start(s32[16]{0:T(128)} %copy-done.41) | copy-start | bytes 196
  141.2 85.3 %copy-start.38 = (s32[64]{0:T(128)S(1)}, s32[64]{0:T(128)}, u32[]{:S(2)}) copy-start(s32[64]{0:T(128)} %copy-done.37) | copy-start | bytes 772
  319.3 76.6 %copy-start.10 = (f32[2,15,64]{2,1,0:T(8,128)S(1)}, f32[2,15,64]{2,1,0:T(8,128)}, u32[]{:S(2)}) copy-start(f32[2,15,64]{2,1,0:T(8,128)} %fusion.73) | copy-start | bytes 23044
  319.3 76.7 %copy-start.16 = (f32[2,16,65]{2,1,0:T(8,128)S(1)}, f32[2,16,65]{2,1,0:T(8,128)}, u32[]{:S(2)}) copy-start(f32[2,16,65]{2,1,0:T(8,128)} %fusion.74) | copy-start | bytes 24964
  321.0 77.2 %copy-start.47 = (f32[3]{0:T(128)S(1)}, f32[3]{0:T(128)}, u32[]{:S(2)}) copy-start(f32[3]{0:T(128)} %constant.123.clone) | copy-start | bytes 40
  321.0 77.2 %copy-start.51 = (f32[3]{0:T(128)S(1)}, f32[3]{0:T(128)}, u32[]{:S(2)}) copy-start(f32[3]{0:T(128)} %constant.124.clone) | copy-start | bytes 40
  396.3 5.2 %collective-permute-start.4 = (f32[10,3,1,1024]{3,0,2,1:T(8,128)S(1)}, f32[10,3,1,1024]{3,0,2,1:T(8,128)S(1)}, u32[]{:S(2)}, u32[]{:S(2)}) collective-permute-start(f32[10,3,1,1024]{3,0,2,1:T(8,128)S(1)} %get-tuple-element.31), channel_id=1, source_target_pairs={{2,0},{4,2},{6,4},{8,6},{10,8},{12,10},{14,12},{16,14},{18,16},{20... | collective-permute-start | bytes 368648 | tf_op jit(solution)/shard_map/ppermute | solution.py:26
  397.4 4.2 collective-permute-start.5
  398.6 16.0 %copy-start.13 = (f32[2,15,64]{2,1,0:T(8,128)S(1)}, f32[2,15,64]{2,1,0:T(8,128)}, u32[]{:S(2)}) copy-start(f32[2,15,64]{2,1,0:T(8,128)} %get-tuple-element.80) | copy-start | bytes 23044
  398.7 16.0 %copy-start.14 = (f32[2,15,64]{2,1,0:T(8,128)S(1)}, f32[2,15,64]{2,1,0:T(8,128)}, u32[]{:S(2)}) copy-start(f32[2,15,64]{2,1,0:T(8,128)} %get-tuple-element.81) | copy-start | bytes 23044
  401.5 10.5 %copy-start.3 = (f32[10,3,1,1024]{3,0,2,1:T(8,128)}, f32[10,3,1,1024]{3,0,2,1:T(8,128)S(1)}, u32[]{:S(2)}) copy-start(f32[10,3,1,1024]{3,0,2,1:T(8,128)S(1)} %collective-permute-done.4) | copy-start | bytes 368644
  401.5 10.5 %copy-start.5 = (f32[10,3,1,1024]{3,0,2,1:T(8,128)}, f32[10,3,1,1024]{3,0,2,1:T(8,128)S(1)}, u32[]{:S(2)}) copy-start(f32[10,3,1,1024]{3,0,2,1:T(8,128)S(1)} %collective-permute-done.5) | copy-start | bytes 368644
  418.8 6.4 %copy-start.23 = (f32[2,1024]{1,0:T(2,128)S(1)}, f32[2,1024]{1,0:T(2,128)}, u32[]{:S(2)}) copy-start(f32[2,1024]{1,0:T(2,128)} %get-tuple-element.39) | copy-start | bytes 24580
  418.8 6.4 %copy-start.24 = (f32[2,1024]{1,0:T(2,128)S(1)}, f32[2,1024]{1,0:T(2,128)}, u32[]{:S(2)}) copy-start(f32[2,1024]{1,0:T(2,128)} %get-tuple-element.40) | copy-start | bytes 24580
  418.8 6.4 %copy-start.25 = (f32[2,1024]{1,0:T(2,128)S(1)}, f32[2,1024]{1,0:T(2,128)}, u32[]{:S(2)}) copy-start(f32[2,1024]{1,0:T(2,128)} %get-tuple-element.41) | copy-start | bytes 24580
  418.8 6.4 %copy-start.28 = (f32[2,1024]{1,0:T(2,128)S(1)}, f32[2,1024]{1,0:T(2,128)}, u32[]{:S(2)}) copy-start(f32[2,1024]{1,0:T(2,128)} %get-tuple-element.35) | copy-start | bytes 24580
  418.8 6.4 %copy-start.29 = (f32[2,1024]{1,0:T(2,128)S(1)}, f32[2,1024]{1,0:T(2,128)}, u32[]{:S(2)}) copy-start(f32[2,1024]{1,0:T(2,128)} %get-tuple-element.36) | copy-start | bytes 24580
  418.8 6.4 %copy-start.30 = (f32[2,1024]{1,0:T(2,128)S(1)}, f32[2,1024]{1,0:T(2,128)}, u32[]{:S(2)}) copy-start(f32[2,1024]{1,0:T(2,128)} %get-tuple-element.37) | copy-start | bytes 24580
  418.8 6.4 %copy-start.44 = (f32[3]{0:T(128)S(1)}, f32[3]{0:T(128)}, u32[]{:S(2)}) copy-start(f32[3]{0:T(128)} %constant.125.clone) | copy-start | bytes 40
  423.9 4.8 copy-start.34
  425.2 2.9 copy-start.36
  425.2 4.1 copy-start.4
  425.2 4.1 copy-start.6
  425.2 4.1 copy-start.22
  425.2 4.1 copy-start.27
  425.3 4.1 copy-start.32
  (15 other events, 20.9 us)
where the time goes:
time: 523 us; the launch traced here: 515 us
  blocking collectives  297 us (57%)
  local copies, waits for them, and re-layouts  110 us (21%)
  other arithmetic  29.1 us (6%)
  waiting for transfers between devices  27.1 us (5%)
  starting transfers between devices  26.3 us (5%)
  matrix products  18.5 us (4%)
  between operations  6.27 us (1%)
    psum x2, blocking collectives, precond_sum(): return lax.psum(jnp.sum(residual * smoothed), ('circ', 'mode'))  154 us
    psum x1, blocking collectives, on_device(): alpha = inner_now / lax.psum(jnp.sum(direction * image), ('circ', 'mode'))  80.2 us
    unnamed x120, local copies, waits for them, and re-layouts  43.9 us
    all_to_all x1, blocking collectives, precondition(): lax.all_to_all(spec, 'circ', split_axis=3, concat_axis=2, tiled=True)  22 us
    all_gather x2, blocking collectives, on_device(): fold_piece = lax.all_gather(padded, 'mode', axis=0, tiled=True)  20.9 us
    all_to_all x1, blocking collectives, spectral(): lax.all_to_all(jnp.swapaxes(restored, 2, 3), 'circ', split_axis=2, concat...  20.3 us
    all_to_all x1, starting transfers between devices, precondition(): lax.all_to_all(spec, 'circ', split_axis=3, concat_axis=2, tiled=True)  14.9 us
    all_to_all x2, local copies, waits for them, and re-layouts, spectral(): lax.all_to_all(jnp.swapaxes(restored, 2, 3), 'circ', split_axis=2, concat...  14 us
  transfers between devices with their start and end apart: 8, of which 6 were waited for; matrix products, arithmetic and copies ran while one was open for 6% of the time, Pallas kernels for 0%

commit v1 on v0

v1 whole, which is shorter than its diff:
```python
import functools
import math

import jax
import jax.numpy as jnp
import numpy as np
from jax import lax
from jax.experimental import pallas as pl
from jax.experimental.pallas import tpu as pltpu
from jax.sharding import PartitionSpec as P

MESH = pl.DeviceIdType.MESH
HIGHEST = lax.Precision.HIGHEST
NC, NL, NT = 256, 16, 64
ROWS = 512
FIELD = (ROWS, 128)
GAMMA = 30
Z_ORDER = (4, 3, 5, 2, 6, 1, 7, 0)

T_FWD, T_INV, T_LAMK, T_LAMT, T_LAML, T_SCALE, T_W, T_SAME, T_MODE = 0, 128, 256, 512, 576, 584, 592, 600, 728


def tables():
    n = np.arange(NC)
    angle = 2.0 * np.pi / NC * ((n[:, None] * n[None, :]) % NC)
    hart = np.cos(angle) + np.sin(angle)
    ell = np.arange(NL)
    cosine = np.cos(np.pi / (2 * NL) * (((2 * ell[:, None] + 1) * ell[None, :]) % (4 * NL)))
    tee = np.arange(NT) + 1
    sine = np.sin(np.pi / (NT + 1) * ((tee[:, None] * tee[None, :]) % (2 * (NT + 1))))
    lane = np.arange(128)
    half, q = lane // 64, lane % 32
    mode, comp, valid = (lane % 64) // 32 * 10 + q // 3, q % 3, q < 30
    weight = [np.where(comp == d, 2.0, 1.0) for d in range(3)]
    table = np.zeros((856, 128))
    for a in range(8):
        for b in range(8):
            table[T_FWD + a * 8 + b] = cosine[half * 8 + b, half * 8 + a]
            table[T_FWD + 64 + a * 8 + b] = cosine[(1 - half) * 8 + b, half * 8 + a]
            table[T_INV + a * 8 + b] = cosine[half * 8 + a, half * 8 + b]
            table[T_INV + 64 + a * 8 + b] = cosine[half * 8 + a, (1 - half) * 8 + b]
    table[T_LAMK : T_LAMK + NC] = (2 - 2 * np.cos(2 * np.pi / NC * n))[:, None] * weight[0]
    table[T_LAMT : T_LAMT + NT] = (2 - 2 * np.cos(np.pi / (NT + 1) * tee))[:, None] * weight[2]
    for a in range(8):
        m = half * 8 + a
        table[T_LAML + a] = (2 - 2 * np.cos(np.pi / NL * m)) * weight[1]
        table[T_SCALE + a] = NC * np.where(m == 0, NL, NL / 2) * (NT + 1) / 2
    for d in range(3):
        table[T_W + d] = weight[d]
    table[T_W + 3] = 1.0 / weight[0]
    table[T_W + 4] = valid
    table[T_W + 5] = mode
    same = (half[:, None] == half) & (comp[:, None] == comp) & valid[:, None] & valid
    table[T_SAME : T_SAME + 128] = 0.5 * same
    table[T_MODE : T_MODE + 128] = mode[:, None]
    spread = np.zeros((8, 512))
    for k in range(4):
        for lh in range(2):
            spread[k * 2 + lh, k * 128 : (k + 1) * 128] = half == lh
    expand = (np.arange(20)[:, None] == mode) & valid
    both = np.concatenate([hart[:, 0::2], hart[:, 1::2]], 0)
    block = np.kron(np.eye(4), sine)
    return [np.asarray(v, np.float32) for v in (hart, both, block, table, spread, expand, expand.T)]


def dot(a, b):
    return jnp.dot(a, b, precision=HIGHEST, preferred_element_type=jnp.float32)


def dot_dims(a, b, ca, cb):
    return lax.dot_general(
        a, b, (((ca,), (cb,)), ((), ())), precision=HIGHEST, preferred_element_type=jnp.float32
    )


def total(v):
    return jnp.sum(jnp.sum(v, axis=0, keepdims=True), axis=1, keepdims=True)


def kernel(
    x_ref, st_ref, pair_ref, coup_ref, h_ref, both_ref, block_ref, tab, spread_ref, expand_ref, expand_t_ref,
    ox_ref, or_ref,
    xp, b_in, a_own, a_all, fsend, frecv, rsend, rrecv, sum_out, sum_in, field, zsib, ext, coef, t0, t123, rest, bt, img,
    gg, dinv, spec, tmp, out_send, out_recv, aj, ssem, rsem,
):
    circ, mode = lax.axis_index("circ"), lax.axis_index("mode")
    me = circ * 2 + mode
    xl, z, y, core = circ // 64, lax.rem(circ // 8, 8), lax.rem(circ // 2, 4), lax.rem(circ, 2)
    chip = circ // 2
    cell = 4 * chip + 2 * mode + core
    lane = lax.broadcasted_iota(jnp.int32, (1, 128), 1)
    low = lane < 64
    gamma_lane = lane == GAMMA
    valid = tab[T_W + 4 : T_W + 5, :] > 0.5

    def everyone(act):
        z_parts = [lax.rem(z + zo, 8) * 8 for zo in Z_ORDER]
        for yo in (2, 1, 3, 0):
            y_part = lax.rem(y + yo, 4) * 2

            def step(i, carry):
                k = 7 - i
                base = lax.rem(xl + k // 4, 2) * 64 + y_part + lax.rem(core + lax.rem(k // 2, 2), 2)
                there = lax.rem(mode + lax.rem(k, 2), 2)
                for part in z_parts:
                    act(base + part, there)
                return carry

            lax.fori_loop(0, 8 if yo else 7, step, 0)
        for part in z_parts[:-1]:
            act(xl * 64 + y * 2 + core + part, mode)

    def remote(src, dst, sem, where):
        pltpu.make_async_remote_copy(
            src_ref=src, dst_ref=dst, send_sem=ssem.at[sem], recv_sem=rsem.at[sem], device_id=where, device_id_type=MESH
        ).start()

    def local(src, dst, sem):
        pltpu.make_async_copy(src, dst, rsem.at[sem]).start()

    def landed(ref, sem):
        pltpu.make_async_copy(ref, ref, rsem.at[sem]).wait()

    def sent(ref, sem):
        pltpu.make_async_copy(ref, ref, ssem.at[sem]).wait()

    def pair_rows(index):
        return pl.ds(pl.multiple_of(index * 2, 2), 2)

    barrier = pltpu.get_barrier_semaphore()
    everyone(lambda c, m: pl.semaphore_signal(barrier, 1, device_id=(c, m), device_id_type=MESH))

    for part in range(4):
        xp[part * 32 + 24 : part * 32 + 32, :] = jnp.zeros((8, 512), jnp.float32)

    def load_row(r, carry):
        for e in range(2):
            for lh in range(2):
                xp[pl.ds(lh * 64 + e * 32 + r, 1), :] = x_ref[r, e : e + 1, lh * 512 : (lh + 1) * 512]
        return carry

    lax.fori_loop(0, 30, load_row, 0)
    for k in range(4):
        for e in range(2):
            for lh in range(2):
                row = k * 2 + lh
                a_own[e, row : row + 1, :] = st_ref[k, e : e + 1, lh * 512 : (lh + 1) * 512]

    def transform_t(src, dst):
        for s in (0, 256):
            dst[s : s + 256, :] = dot(block_ref[...], src[s : s + 256, :])

    def transform_l(src, dst, base, fill=None):
        def chunk(i, carry):
            at = pl.multiple_of(i * 16, 16)
            held = [src[pl.ds(at + j * 64, 16), :] for j in range(8)]
            turned = [pltpu.roll(v, 64, 1) for v in held]
            for a in range(8):
                acc = None
                for b in range(8):
                    row = base + a * 8 + b
                    term = tab[row : row + 1, :] * held[b] + tab[row + 64 : row + 65, :] * turned[b]
                    acc = term if acc is None else acc + term
                if fill is not None:
                    acc = jnp.where(gamma_lane, fill, acc)
                dst[pl.ds(at + a * 64, 16), :] = acc
            return carry

        lax.fori_loop(0, 4, chunk, 0)

    tmp[...] = jnp.transpose(xp[...])
    transform_t(tmp, t0)
    transform_l(t0, fsend.at[0], T_FWD)

    pl.semaphore_wait(barrier, 255)

    my_rows = pair_rows(mode * 128 + circ)
    everyone(lambda c, m: remote(fsend.at[0, pair_rows(c * 2 + m)], frecv.at[0, my_rows], 0, (c, m)))
    local(fsend.at[0, pair_rows(me)], frecv.at[0, my_rows], 0)

    sibling = (chip * 2 + 1 - core, mode)
    own_slot = 1 + 2 * core
    remote(a_own, a_all.at[pl.ds(own_slot, 2)], 9, sibling)
    a_all[pl.ds(own_slot, 2)] = a_own[...]
    beside = lax.rem(chip + 63 + 2 * core, 64)
    for e in range(2):
        remote(a_own.at[core], a_all.at[5 - 5 * core], 9, (beside * 2 + e, mode))
    for e in range(2):
        itself = jnp.logical_and(core == e, mode == core)
        for lh in range(2):
            src = xp.at[pl.ds(lh * 64 + e * 32, 32)]
            dst = b_in.at[pl.ds(pl.multiple_of(lh * 64 + mode * 32, 32), 32)]

            @pl.when(itself)
            def _():
                local(src, dst, 8)

            @pl.when(jnp.logical_not(itself))
            def _():
                remote(src, dst, 8, (chip * 2 + e, core))

    row_m = me // 32
    mu_l = tab[pl.ds(T_LAML + row_m, 1), :]
    scale = tab[pl.ds(T_SCALE + row_m, 1), :]
    for r in range(2):
        mu = mu_l + tab[pl.ds(T_LAMT + 2 * lax.rem(me, 32) + r, 1), :]
        dinv[:, r * 128 : (r + 1) * 128] = 1.0 / ((tab[T_LAMK : T_LAMK + 256, :] + mu) * scale)
    pairing = pair_ref[...].astype(jnp.float32)
    coupling = coup_ref[...]
    pair_row, coup_row = dot(pairing, expand_ref[...]), dot(coupling, expand_ref[...])
    pair_col, coup_col = dot_dims(expand_t_ref[...], pairing, 1, 1), dot_dims(expand_t_ref[...], coupling, 1, 1)
    mode_row, mode_col = tab[T_W + 5 : T_W + 6, :], tab[T_MODE : T_MODE + 128, :]
    for k in range(3):
        forth = jnp.where(jnp.abs(pair_col[:, k : k + 1] - mode_row) < 0.5, coup_col[:, k : k + 1], 0.0)
        back = jnp.where(jnp.abs(pair_row[k : k + 1, :] - mode_col) < 0.5, coup_row[k : k + 1, :], 0.0)
        gg[k * 128 : (k + 1) * 128, :] = tab[T_SAME : T_SAME + 128, :] * (forth + back)

    lane2 = lax.broadcasted_iota(jnp.int32, (1, 256), 1)
    first = lax.rem(lane2 // 32, 2) == 0
    real = lax.rem(lane2, 32) < 30

    def back_to_cells(sem, carried):
        weighted = spec[...] * dinv[...]
        own = total(spec[...] * weighted)
        cells = jnp.where(lane2 == GAMMA, own, dot(h_ref[...], weighted))
        for r in range(2):
            rsend[carried, pl.ds(r, 256, stride=2), :] = cells[:, r * 128 : (r + 1) * 128]
        mine = pair_rows(me)

        def act(c, m):
            there = 4 * (c // 2) + 2 * m + lax.rem(c, 2)
            remote(rsend.at[carried, pair_rows(there)], rrecv.at[carried, mine], sem, (c, m))

        everyone(act)
        local(rsend.at[carried, pair_rows(cell)], rrecv.at[carried, mine], sem)

    landed(frecv.at[0], 0)
    parts = []
    for hh in range(2):
        both = jnp.concatenate([frecv[0, pl.ds(hh * 256 + r, 128, stride=2), :] for r in range(2)], 1)
        parts.append(dot(both_ref[...], both))
    spec[...] = jnp.where(
        first,
        parts[0][:256] + pltpu.roll(parts[0][256:], 224, 1),
        parts[1][256:] + pltpu.roll(parts[1][:256], 32, 1),
    )
    back_to_cells(1, 0)

    def turned_ends(src, dst):
        dst[64:576, :] = src
        dst[0:64, :] = pltpu.roll(src[448:512], 64, 1)
        dst[576:640, :] = pltpu.roll(src[0:64], 64, 1)

    w0, w1, w2, iw0 = [tab[T_W + d : T_W + d + 1, :] for d in range(4)]
    row64 = lax.broadcasted_iota(jnp.int32, (64, 128), 0)
    lane64 = lax.broadcasted_iota(jnp.int32, (64, 128), 1)
    landed(a_all.at[pl.ds(0, 4)], 9)
    slot = 1 + 2 * mode + core
    for which, at in enumerate((slot, slot + 1 - 2 * core, slot - 1 + 2 * core)):
        aj[which] = dot_dims(a_all[at], spread_ref[...], 0, 0)
    for k in range(4):
        turned_ends(aj[0, :, k * 128 : (k + 1) * 128], ext)

        def faces(g, carry):
            at = pl.multiple_of(g * 64, 64)
            here = pl.ds(at, 64)
            a = ext[pl.ds(at + 64, 64), :]
            up, down = ext[pl.ds(at + 128, 64), :], ext[pl.ds(at, 64), :]
            sib, oth = aj[1, here, k * 128 : (k + 1) * 128], aj[2, here, k * 128 : (k + 1) * 128]
            tp = jnp.where(row64 == 63, a, pltpu.roll(a, 63, 0))
            tm = jnp.where(row64 == 0, a, pltpu.roll(a, 1, 0))
            last = jnp.logical_and(g == 7, lane64 >= 64)
            start = jnp.logical_and(g == 0, lane64 < 64)
            coef[k * 6, here, :] = (0.5 * w0) * (a + sib)
            coef[k * 6 + 1, here, :] = (0.5 * w0) * (a + oth)
            coef[k * 6 + 2, here, :] = jnp.where(last, 0.0, (0.5 * w1) * (a + up))
            coef[k * 6 + 3, here, :] = jnp.where(start, 0.0, (0.5 * w1) * (a + down))
            coef[k * 6 + 4, here, :] = (0.5 * w2) * (a + tp)
            coef[k * 6 + 5, here, :] = (0.5 * w2) * (a + tm)
            return carry

        lax.fori_loop(0, 8, faces, 0)
    landed(b_in, 8)
    bt[...] = jnp.transpose(b_in[...])

    def smoothed(n):
        landed(rrecv.at[n], 1 + 2 * n)
        carried = jnp.sum(jnp.sum(rrecv[n], axis=0, keepdims=True) * jnp.where(gamma_lane, 1.0, 0.0), axis=1, keepdims=True)
        transform_l(rrecv.at[n], tmp, T_INV)
        for s in (0, 256):
            field[n, s : s + 256, :] = jnp.where(valid, dot(block_ref[...], tmp[s : s + 256, :]), 0.0)
        remote(field.at[n], zsib.at[n], 5 + n, sibling)
        return carried

    def operator(n):
        turned_ends(field[n], ext)

        def inner(g, carry):
            at = pl.multiple_of(g * 64, 64)
            here = pl.ds(at, 64)
            v = ext[pl.ds(at + 64, 64), :]
            lp, lm = v - ext[pl.ds(at + 128, 64), :], v - ext[pl.ds(at, 64), :]
            tp = v - jnp.where(row64 == 63, 0.0, pltpu.roll(v, 63, 0))
            tm = v - jnp.where(row64 == 0, 0.0, pltpu.roll(v, 1, 0))
            for k in range(4):
                acc = (
                    coef[k * 6 + 2, here, :] * lp
                    + coef[k * 6 + 3, here, :] * lm
                    + coef[k * 6 + 4, here, :] * tp
                    + coef[k * 6 + 5, here, :] * tm
                )
                if k:
                    t123[here, (k - 1) * 128 : k * 128] = acc
                else:
                    t0[here, :] = acc
            last = jnp.logical_and(g == 7, lane64 >= 64)
            start = jnp.logical_and(g == 0, lane64 < 64)
            lap = w1 * (jnp.where(last, 0.0, lp) + jnp.where(start, 0.0, lm)) + w2 * (tp + tm) - bt[here, :]
            rest[here, :] = -(v + iw0 * lap)
            return carry

        lax.fori_loop(0, 8, inner, 0)
        landed(zsib.at[n], 5 + n)

        def outer(g, carry):
            here = pl.ds(pl.multiple_of(g * 64, 64), 64)
            sib = zsib[n, here, :]
            one, two = field[n, here, :] - sib, sib + rest[here, :]
            for k in range(4):
                acc = coef[k * 6, here, :] * one + coef[k * 6 + 1, here, :] * two
                if k:
                    t123[here, (k - 1) * 128 : k * 128] += acc
                else:
                    t0[here, :] += acc
            return carry

        lax.fori_loop(0, 8, outer, 0)
        img[n] = t0[...] + dot(t123[...], gg[...])

    def to_home(f):
        for hh in range(2):
            itself = jnp.logical_and(core == mode, mode == hh)
            for lh in range(2):
                src = out_send.at[f, pl.ds(lh * 64 + hh * 32, 32)]
                dst = out_recv.at[f, pl.ds(pl.multiple_of(lh * 64 + core * 32, 32), 32)]

                @pl.when(itself)
                def _():
                    local(src, dst, 10 + f)

                @pl.when(jnp.logical_not(itself))
                def _():
                    remote(src, dst, 10 + f, (chip * 2 + mode, hh))

    rz0 = smoothed(0)
    operator(0)
    dad = total(field[0] * img[0])

    transform_t(img.at[0], tmp)
    transform_l(tmp, fsend.at[1], T_FWD, fill=dad)
    cell_rows = pair_rows(cell)
    everyone(lambda c, m: remote(fsend.at[1, pair_rows(c * 2 + m)], frecv.at[1, cell_rows], 2, (c, m)))
    local(fsend.at[1, pair_rows(me)], frecv.at[1, cell_rows], 2)
    out_send[0] = jnp.transpose(field[0])
    to_home(0)
    out_send[1] = jnp.transpose(img[0])
    to_home(1)

    landed(frecv.at[1], 2)
    even = frecv[1, pl.ds(0, 256, stride=2), :]
    sums = jnp.sum(even, axis=0, keepdims=True)
    dad = jnp.sum(jnp.where(gamma_lane, sums, 0.0), axis=1, keepdims=True)
    alpha0 = rz0 / dad
    image_spec = dot(h_ref[...], jnp.concatenate([even, frecv[1, pl.ds(1, 256, stride=2), :]], 1))
    spec[...] = jnp.where(real, spec[...] - alpha0 * image_spec, 0.0)
    back_to_cells(3, 1)
    bt[...] = bt[...] - alpha0 * img[0]

    rz1 = smoothed(1)
    beta = rz1 / rz0
    operator(1)
    dad = total((field[1] + beta * field[0]) * (img[1] + beta * img[0]))
    sum_out[...] = jnp.broadcast_to(dad, (8, 128))
    sum_in[pl.ds(me, 1), :] = jnp.broadcast_to(dad, (1, 128))
    everyone(lambda c, m: remote(sum_out.at[pl.ds(0, 1)], sum_in.at[pl.ds(me, 1)], 4, (c, m)))
    out_send[2] = jnp.transpose(field[1])
    to_home(2)
    out_send[3] = jnp.transpose(img[1])
    to_home(3)
    landed(sum_in.at[pl.ds(0, 255)], 4)
    alpha1 = rz1 / jnp.sum(sum_in[...], axis=0, keepdims=True)[:, :1]
    both_steps = alpha0 + alpha1 * beta
    for f in range(4):
        landed(out_recv.at[f], 10 + f)
    out_recv[0] = both_steps * out_recv[0] + alpha1 * out_recv[2]
    out_recv[1] = xp[...] - both_steps * out_recv[1] - alpha1 * out_recv[3]

    def store_row(r, carry):
        for e in range(2):
            for lh in range(2):
                row = pl.ds(lh * 64 + e * 32 + r, 1)
                ox_ref[r, e : e + 1, lh * 512 : (lh + 1) * 512] = out_recv[0, row, :]
                or_ref[r, e : e + 1, lh * 512 : (lh + 1) * 512] = out_recv[1, row, :]
        return carry

    lax.fori_loop(0, 30, store_row, 0)

    for n in range(2):
        sent(fsend.at[n, pl.ds(0, 510)], 2 * n)
        sent(rsend.at[n, pl.ds(0, 510)], 1 + 2 * n)
        sent(field.at[n], 5 + n)
    sent(sum_in.at[pl.ds(0, 255)], 4)
    sent(a_all.at[pl.ds(0, 4)], 9)

    @pl.when(core == mode)
    def _():
        sent(xp.at[pl.ds(0, 64)], 8)
        for f in range(4):
            sent(out_send.at[f, pl.ds(0, 64)], 10 + f)

    @pl.when(core != mode)
    def _():
        sent(xp, 8)
        for f in range(4):
            sent(out_send.at[f], 10 + f)


def on_device(right_side, stiffness, pairing, coupling):
    consts = [jnp.asarray(v) for v in tables()]
    shape = jax.ShapeDtypeStruct((30, 2, 1024), jnp.float32)
    vmem = pl.BlockSpec(memory_space=pltpu.VMEM)
    f32 = jnp.float32
    scratch = [
        pltpu.VMEM((128, 512), f32),
        pltpu.VMEM((128, 512), f32),
        pltpu.VMEM((2, 8, 512), f32),
        pltpu.VMEM((6, 8, 512), f32),
        pltpu.VMEM((2,) + FIELD, f32),
        pltpu.VMEM((2,) + FIELD, f32),
        pltpu.VMEM((2,) + FIELD, f32),
        pltpu.VMEM((2,) + FIELD, f32),
        pltpu.VMEM((8, 128), f32),
        pltpu.VMEM((256, 128), f32),
        pltpu.VMEM((2,) + FIELD, f32),
        pltpu.VMEM((2,) + FIELD, f32),
        pltpu.VMEM((640, 128), f32),
        pltpu.VMEM((24,) + FIELD, f32),
        pltpu.VMEM(FIELD, f32),
        pltpu.VMEM((512, 384), f32),
        pltpu.VMEM(FIELD, f32),
        pltpu.VMEM(FIELD, f32),
        pltpu.VMEM((2,) + FIELD, f32),
        pltpu.VMEM((384, 128), f32),
        pltpu.VMEM((256, 256), f32),
        pltpu.VMEM((256, 256), f32),
        pltpu.VMEM(FIELD, f32),
        pltpu.VMEM((4, 128, 512), f32),
        pltpu.VMEM((4, 128, 512), f32),
        pltpu.VMEM((3, 512, 512), f32),
        pltpu.SemaphoreType.DMA((14,)),
        pltpu.SemaphoreType.DMA((14,)),
    ]
    x, r = pl.pallas_call(
        kernel,
        out_shape=(shape, shape),
        in_specs=[vmem] * 11,
        out_specs=(vmem, vmem),
        scratch_shapes=scratch,
        compiler_params=pltpu.CompilerParams(
            collective_id=0, has_side_effects=True, vmem_limit_bytes=44 * 1024 * 1024
        ),
    )(right_side.reshape(30, 2, 1024), stiffness, pairing, coupling, *consts)
    return x.reshape(right_side.shape), r.reshape(right_side.shape)


def solution(mesh):
    placed = P("mode", None, "circ", None)
    return jax.shard_map(
        on_device,
        mesh=mesh,
        in_specs=(placed, P(None, "circ", None), P(), P()),
        out_specs=(placed, placed),
        check_vma=False,
    )
```

time: 523 us -> 90 us (0.17); the launches traced: 515 us -> 89.5 us
  blocking collectives: 297 us -> 0 us
  local copies, waits for them, and re-layouts: 110 us -> 10.6 us
  Pallas kernels: 0 us -> 78.3 us
  other arithmetic: 29.1 us -> 0 us
  waiting for transfers between devices: 27.1 us -> 0 us
  starting transfers between devices: 26.3 us -> 0 us
  matrix products: 18.5 us -> 0 us
  between operations: 6.27 us -> 0.66 us
    psum x3 -> x0, blocking collectives: 234 us -> none  [the longest x2 154 us: precond_sum(): return lax.psum(jnp.sum(residual * smoothed), ('circ', 'mode'))]
    pallas_call x0 -> x1, Pallas kernels: none -> 78.3 us  [on_device(): pl.pallas_call(kernel, out_shape=(shape, shape), in_specs=[vmem] * 11, ou...]
    all_to_all x2 -> x0, blocking collectives: 42.4 us -> none  [the longest x1 22 us: precondition(): lax.all_to_all(spec, 'circ', split_axis=3, concat_axis=2, tiled=True)]
    unnamed x120 -> x24, local copies, waits for them, and re-layouts: 43.9 us -> 10.6 us
    reshape x23 -> x0, local copies, waits for them, and re-layouts: 33.3 us -> none  [the longest x8 13.8 us: stencil(): inner.reshape(num_modes, num_comps, span, num_cells)]
    all_to_all x7 -> x0, local copies, waits for them, and re-layouts: 25.1 us -> none  [the longest x2 14 us: spectral(): lax.all_to_all(jnp.swapaxes(restored, 2, 3), 'circ', split_axis=2, concat...]
    all_to_all x2 -> x0, starting transfers between devices: 21.6 us -> none  [the longest x1 14.9 us: precondition(): lax.all_to_all(spec, 'circ', split_axis=3, concat_axis=2, tiled=True)]
    all_to_all x2 -> x0, waiting for transfers between devices: 21.4 us -> none  [the longest x1 13.2 us: spectral(): lax.all_to_all(jnp.swapaxes(restored, 2, 3), 'circ', split_axis=2, concat...]
  transfers between devices with their start and end apart: 8 -> 0, of which waited for: 6 -> 0; matrix products, arithmetic and copies ran while one was open for 6% -> 0% of each run, Pallas kernels for 0% -> 0%
where the time goes in v1:
time: 90 us; the launch traced here: 89.5 us
  Pallas kernels  78.3 us (87%)
  local copies, waits for them, and re-layouts  10.6 us (12%)
    pallas_call x1, Pallas kernels, on_device(): pl.pallas_call(kernel, out_shape=(shape, shape), in_specs=[vmem] * 11, ou...  78.3 us
    unnamed x24, local copies, waits for them, and re-layouts  10.6 us

profile of v1, /device:TPU:1, one launch (start us, length us, event | category | flops | bytes accessed | tf_op | source)
XLA Modules:
  0.0 89.5 jit_solution(7747028837856954900)
XLA Ops:
  0.6 0.0 copy-start
  0.6 1.0 %copy-done = f32[856,128]{1,0:T(8,128)S(1)} copy-done((f32[856,128]{1,0:T(8,128)S(1)}, f32[856,128]{1,0:T(8,128)}, u32[]{:S(2)}) %copy-start) | copy-done | bytes 438296
  1.6 0.0 copy-start.1
  1.6 0.9 %copy-done.1 = f32[256,256]{1,0:T(8,128)S(1)} copy-done((f32[256,256]{1,0:T(8,128)S(1)}, f32[256,256]{1,0:T(8,128)}, u32[]{:S(2)}) %copy-start.1) | copy-done | bytes 262168
  2.6 0.0 copy-start.2
  2.6 0.9 %copy-done.2 = f32[512,128]{1,0:T(8,128)S(1)} copy-done((f32[512,128]{1,0:T(8,128)S(1)}, f32[512,128]{1,0:T(8,128)}, u32[]{:S(2)}) %copy-start.2) | copy-done | bytes 262168
  3.5 0.0 copy-start.3
  3.5 0.9 %copy-done.3 = f32[256,256]{1,0:T(8,128)S(1)} copy-done((f32[256,256]{1,0:T(8,128)S(1)}, f32[256,256]{1,0:T(8,128)}, u32[]{:S(2)}) %copy-start.3) | copy-done | bytes 262168
  4.5 0.0 copy-start.4
  4.5 0.9 %copy-done.4 = f32[10,3,2,1024]{3,2,1,0:T(2,128)S(1)} copy-done((f32[10,3,2,1024]{3,2,1,0:T(2,128)S(1)}, f32[10,3,2,1024]{3,2,1,0:T(2,128)}, u32[]{:S(2)}) %copy-start.4) | copy-done | bytes 245784
  5.4 0.0 copy-start.5
  5.4 0.8 copy-done.5
  6.3 0.0 copy-start.6
  6.3 0.8 copy-done.6
  7.0 0.0 copy-start.7
  7.0 0.7 copy-done.7
  7.8 0.0 copy-start.8
  7.8 0.7 copy-done.8
  8.5 0.0 copy-start.9
  8.5 0.7 copy-done.9
  9.1 0.0 copy-start.10
  9.2 0.7 copy-done.10
  9.8 78.3 %shard_map.122 = (f32[30,2,1024]{2,1,0:T(2,128)S(1)}, f32[30,2,1024]{2,1,0:T(2,128)S(1)}) custom-call(f32[30,2,1024]{2,1,0:T(2,128)S(1)} %bitcast.3, f32[4,2,1024]{2,1,0:T(2,128)S(1)} %copy-done.6, s32[3,20]{1,0:T(4,128)S(1)} %copy-done.9, f32[3,20]{1,0:T(4,128)S(1)} %copy-done.10, f32[256,256]{1,0:T(8,128)S(1)} %copy-done.3, f32[512,128]{1,0:T(8,128)S(1)} %copy-done.2, ...), custom_call_target="tpu_custom_call" | custom-call | tf_op jit(solution)/shard_map/pallas_call | solution.py:463
  88.1 0.7 copy.15
  88.8 0.7 copy.16
Async XLA Ops:
  0.6 1.0 %copy-start = (f32[856,128]{1,0:T(8,128)S(1)}, f32[856,128]{1,0:T(8,128)}, u32[]{:S(2)}) copy-start(f32[856,128]{1,0:T(8,128)} %constant.17.clone.tab) | copy-start | bytes 1314820
  1.6 0.9 %copy-start.1 = (f32[256,256]{1,0:T(8,128)S(1)}, f32[256,256]{1,0:T(8,128)}, u32[]{:S(2)}) copy-start(f32[256,256]{1,0:T(8,128)} %constant.16.clone.block_ref) | copy-start | bytes 786436
  2.6 0.9 %copy-start.2 = (f32[512,128]{1,0:T(8,128)S(1)}, f32[512,128]{1,0:T(8,128)}, u32[]{:S(2)}) copy-start(f32[512,128]{1,0:T(8,128)} %constant.15.clone.both_ref) | copy-start | bytes 786436
  3.5 0.9 %copy-start.3 = (f32[256,256]{1,0:T(8,128)S(1)}, f32[256,256]{1,0:T(8,128)}, u32[]{:S(2)}) copy-start(f32[256,256]{1,0:T(8,128)} %constant.14.clone.h_ref) | copy-start | bytes 786436
  4.5 0.9 %copy-start.4 = (f32[10,3,2,1024]{3,2,1,0:T(2,128)S(1)}, f32[10,3,2,1024]{3,2,1,0:T(2,128)}, u32[]{:S(2)}) copy-start(f32[10,3,2,1024]{3,2,1,0:T(2,128)} %param.11) | copy-start | bytes 737284
  5.4 0.8 copy-start.5
  6.3 0.8 copy-start.6
  7.0 0.7 copy-start.7
  7.8 0.7 copy-start.8
  8.5 0.7 copy-start.9
  9.1 0.7 copy-start.10

commit v2 on v1

--- a/solution.py
+++ b/solution.py
@@ -17,7 +17,7 @@
 GAMMA = 30
 Z_ORDER = (4, 3, 5, 2, 6, 1, 7, 0)
 
-T_FWD, T_INV, T_LAMK, T_LAMT, T_LAML, T_SCALE, T_W, T_SAME, T_MODE = 0, 128, 256, 512, 576, 584, 592, 600, 728
+T_COS, T_LAMK, T_LAMT, T_LAML, T_SCALE, T_W, T_SAME, T_MODE = 0, 64, 320, 384, 392, 400, 408, 536
 
 
 def tables():
@@ -32,17 +32,14 @@
     half, q = lane // 64, lane % 32
     mode, comp, valid = (lane % 64) // 32 * 10 + q // 3, q % 3, q < 30
     weight = [np.where(comp == d, 2.0, 1.0) for d in range(3)]
-    table = np.zeros((856, 128))
+    table = np.zeros((664, 128))
     for a in range(8):
         for b in range(8):
-            table[T_FWD + a * 8 + b] = cosine[half * 8 + b, half * 8 + a]
-            table[T_FWD + 64 + a * 8 + b] = cosine[(1 - half) * 8 + b, half * 8 + a]
-            table[T_INV + a * 8 + b] = cosine[half * 8 + a, half * 8 + b]
-            table[T_INV + 64 + a * 8 + b] = cosine[half * 8 + a, (1 - half) * 8 + b]
+            table[T_COS + a * 8 + b] = cosine[b, 2 * a + half]
     table[T_LAMK : T_LAMK + NC] = (2 - 2 * np.cos(2 * np.pi / NC * n))[:, None] * weight[0]
     table[T_LAMT : T_LAMT + NT] = (2 - 2 * np.cos(np.pi / (NT + 1) * tee))[:, None] * weight[2]
     for a in range(8):
-        m = half * 8 + a
+        m = 2 * a + half
         table[T_LAML + a] = (2 - 2 * np.cos(np.pi / NL * m)) * weight[1]
         table[T_SCALE + a] = NC * np.where(m == 0, NL, NL / 2) * (NT + 1) / 2
     for d in range(3):
@@ -58,13 +55,17 @@
         for lh in range(2):
             spread[k * 2 + lh, k * 128 : (k + 1) * 128] = half == lh
     expand = (np.arange(20)[:, None] == mode) & valid
-    both = np.concatenate([hart[:, 0::2], hart[:, 1::2]], 0)
+    both = np.concatenate([hart[:, 0::2], hart[:, 1::2]], 1)
     block = np.kron(np.eye(4), sine)
     return [np.asarray(v, np.float32) for v in (hart, both, block, table, spread, expand, expand.T)]
 
 
 def dot(a, b):
     return jnp.dot(a, b, precision=HIGHEST, preferred_element_type=jnp.float32)
+
+
+def dot16(a, b):
+    return jnp.dot(a, b, preferred_element_type=jnp.float32)
 
 
 def dot_dims(a, b, ca, cb):
@@ -78,11 +79,22 @@
 
 
 def kernel(
+    x_far, st_far, pair_far, coup_far, h_far, both_far, block_far, tab_far, spread_far, expand_far, expand_t_far,
+    y_ref,
     x_ref, st_ref, pair_ref, coup_ref, h_ref, both_ref, block_ref, tab, spread_ref, expand_ref, expand_t_ref,
-    ox_ref, or_ref,
     xp, b_in, a_own, a_all, fsend, frecv, rsend, rrecv, sum_out, sum_in, field, zsib, ext, coef, t0, t123, rest, bt, img,
-    gg, dinv, spec, tmp, out_send, out_recv, aj, ssem, rsem,
+    t_high, t_low, gg, dinv, spec, tmp, out_send, out_recv, aj, ssem, rsem, isem,
 ):
+    fetches = {}
+    for n, (src, dst) in enumerate(
+        (
+            (x_far, x_ref), (st_far, st_ref), (block_far, block_ref), (tab_far, tab), (pair_far, pair_ref), (coup_far, coup_ref),
+            (expand_far, expand_ref), (expand_t_far, expand_t_ref), (both_far, both_ref), (h_far, h_ref), (spread_far, spread_ref),
+        )
+    ):
+        fetches[n] = pltpu.make_async_copy(src, dst, isem.at[n])
+        fetches[n].start()
+
     circ, mode = lax.axis_index("circ"), lax.axis_index("mode")
     me = circ * 2 + mode
     xl, z, y, core = circ // 64, lax.rem(circ // 8, 8), lax.rem(circ // 2, 4), lax.rem(circ, 2)
@@ -91,7 +103,7 @@
     lane = lax.broadcasted_iota(jnp.int32, (1, 128), 1)
     low = lane < 64
     gamma_lane = lane == GAMMA
-    valid = tab[T_W + 4 : T_W + 5, :] > 0.5
+    valid = lax.rem(lane, 32) < 30
 
     def everyone(act):
         z_parts = [lax.rem(z + zo, 8) * 8 for zo in Z_ORDER]
@@ -130,6 +142,8 @@
     barrier = pltpu.get_barrier_semaphore()
     everyone(lambda c, m: pl.semaphore_signal(barrier, 1, device_id=(c, m), device_id_type=MESH))
 
+    fetches[0].wait()
+    fetches[1].wait()
     for part in range(4):
         xp[part * 32 + 24 : part * 32 + 32, :] = jnp.zeros((8, 512), jnp.float32)
 
@@ -146,31 +160,53 @@
                 row = k * 2 + lh
                 a_own[e, row : row + 1, :] = st_ref[k, e : e + 1, lh * 512 : (lh + 1) * 512]
 
+    def sines(src):
+        return dot(block_ref[...], jnp.concatenate([src[0:256, :], src[256:512, :]], 1))
+
     def transform_t(src, dst):
-        for s in (0, 256):
-            dst[s : s + 256, :] = dot(block_ref[...], src[s : s + 256, :])
-
-    def transform_l(src, dst, base, fill=None):
+        out = sines(src)
+        dst[0:256, :] = out[:, :128]
+        dst[256:512, :] = out[:, 128:]
+
+    def cosines_forward(src, dst, fill=None):
         def chunk(i, carry):
             at = pl.multiple_of(i * 16, 16)
             held = [src[pl.ds(at + j * 64, 16), :] for j in range(8)]
             turned = [pltpu.roll(v, 64, 1) for v in held]
+            folded = [jnp.where(low, held[j] + turned[7 - j], turned[j] - held[7 - j]) for j in range(8)]
             for a in range(8):
-                acc = None
-                for b in range(8):
-                    row = base + a * 8 + b
-                    term = tab[row : row + 1, :] * held[b] + tab[row + 64 : row + 65, :] * turned[b]
-                    acc = term if acc is None else acc + term
+                acc = tab[T_COS + a * 8 : T_COS + a * 8 + 1, :] * folded[0]
+                for b in range(1, 8):
+                    acc = acc + tab[T_COS + a * 8 + b : T_COS + a * 8 + b + 1, :] * folded[b]
                 if fill is not None:
                     acc = jnp.where(gamma_lane, fill, acc)
                 dst[pl.ds(at + a * 64, 16), :] = acc
             return carry
 
-        lax.fori_loop(0, 4, chunk, 0)
+        lax.fori_loop(0, 4, chunk, 0, unroll=True)
+
+    def cosines_back(src, dst):
+        def chunk(i, carry):
+            at = pl.multiple_of(i * 16, 16)
+            held = [src[pl.ds(at + j * 64, 16), :] for j in range(8)]
+            folded, turned = [], []
+            for b in range(8):
+                acc = tab[T_COS + b : T_COS + b + 1, :] * held[0]
+                for a in range(1, 8):
+                    acc = acc + tab[T_COS + a * 8 + b : T_COS + a * 8 + b + 1, :] * held[a]
+                folded.append(acc)
+                turned.append(pltpu.roll(acc, 64, 1))
+            for b in range(8):
+                dst[pl.ds(at + b * 64, 16), :] = jnp.where(low, folded[b] + turned[b], turned[7 - b] - folded[7 - b])
+            return carry
+
+        lax.fori_loop(0, 4, chunk, 0, unroll=True)
 
     tmp[...] = jnp.transpose(xp[...])
+    for n in range(2, 11):
+        fetches[n].wait()
     transform_t(tmp, t0)
-    transform_l(t0, fsend.at[0], T_FWD)
+    cosines_forward(t0, fsend.at[0])
 
     pl.semaphore_wait(barrier, 255)
 
@@ -213,7 +249,10 @@
     for k in range(3):
         forth = jnp.where(jnp.abs(pair_col[:, k : k + 1] - mode_row) < 0.5, coup_col[:, k : k + 1], 0.0)
         back = jnp.where(jnp.abs(pair_row[k : k + 1, :] - mode_col) < 0.5, coup_row[k : k + 1, :], 0.0)
-        gg[k * 128 : (k + 1) * 128, :] = tab[T_SAME : T_SAME + 128, :] * (forth + back)
+        whole = tab[T_SAME : T_SAME + 128, :] * (forth + back)
+        high = whole.astype(jnp.bfloat16)
+        gg[k * 128 : (k + 1) * 128, :128] = high
+        gg[k * 128 : (k + 1) * 128, 128:] = (whole - high.astype(jnp.float32)).astype(jnp.bfloat16)
 
     lane2 = lax.broadcasted_iota(jnp.int32, (1, 256), 1)
     first = lax.rem(lane2 // 32, 2) == 0
@@ -235,15 +274,12 @@
         local(rsend.at[carried, pair_rows(cell)], rrecv.at[carried, mine], sem)
 
     landed(frecv.at[0], 0)
-    parts = []
-    for hh in range(2):
-        both = jnp.concatenate([frecv[0, pl.ds(hh * 256 + r, 128, stride=2), :] for r in range(2)], 1)
-        parts.append(dot(both_ref[...], both))
-    spec[...] = jnp.where(
-        first,
-        parts[0][:256] + pltpu.roll(parts[0][256:], 224, 1),
-        parts[1][256:] + pltpu.roll(parts[1][:256], 32, 1),
-    )
+    arrived = [
+        jnp.concatenate([frecv[0, pl.ds(hh * 256 + r, 128, stride=2), :] for r in range(2)], 1) for hh in range(2)
+    ]
+    even = jnp.where(first, arrived[0], pltpu.roll(arrived[1], 32, 1))
+    odd = jnp.where(first, pltpu.roll(arrived[0], 224, 1), arrived[1])
+    spec[...] = dot(both_ref[...], jnp.concatenate([even, odd], 0))
     back_to_cells(1, 0)
 
     def turned_ends(src, dst):
@@ -286,9 +322,10 @@
     def smoothed(n):
         landed(rrecv.at[n], 1 + 2 * n)
         carried = jnp.sum(jnp.sum(rrecv[n], axis=0, keepdims=True) * jnp.where(gamma_lane, 1.0, 0.0), axis=1, keepdims=True)
-        transform_l(rrecv.at[n], tmp, T_INV)
-        for s in (0, 256):
-            field[n, s : s + 256, :] = jnp.where(valid, dot(block_ref[...], tmp[s : s + 256, :]), 0.0)
+        cosines_back(rrecv.at[n], tmp)
+        out = sines(tmp)
+        for s in range(2):
+            field[n, s * 256 : (s + 1) * 256, :] = jnp.where(valid, out[:, s * 128 : (s + 1) * 128], 0.0)
         remote(field.at[n], zsib.at[n], 5 + n, sibling)
         return carried
 
@@ -319,23 +356,25 @@
             rest[here, :] = -(v + iw0 * lap)
             return carry
 
-        lax.fori_loop(0, 8, inner, 0)
+        lax.fori_loop(0, 8, inner, 0, unroll=True)
         landed(zsib.at[n], 5 + n)
 
         def outer(g, carry):
             here = pl.ds(pl.multiple_of(g * 64, 64), 64)
             sib = zsib[n, here, :]
             one, two = field[n, here, :] - sib, sib + rest[here, :]
-            for k in range(4):
-                acc = coef[k * 6, here, :] * one + coef[k * 6 + 1, here, :] * two
-                if k:
-                    t123[here, (k - 1) * 128 : k * 128] += acc
-                else:
-                    t0[here, :] += acc
+            t0[here, :] += coef[0, here, :] * one + coef[1, here, :] * two
+            for k in range(1, 4):
+                at = slice((k - 1) * 128, k * 128)
+                acc = t123[here, at] + coef[k * 6, here, :] * one + coef[k * 6 + 1, here, :] * two
+                high = acc.astype(jnp.bfloat16)
+                t_high[here, at] = high
+                t_low[here, at] = (acc - high.astype(jnp.float32)).astype(jnp.bfloat16)
             return carry
 
-        lax.fori_loop(0, 8, outer, 0)
-        img[n] = t0[...] + dot(t123[...], gg[...])
+        lax.fori_loop(0, 8, outer, 0, unroll=True)
+        large = dot16(t_high[...], gg[...])
+        img[n] = t0[...] + (large[:, :128] + (large[:, 128:] + dot16(t_low[...], gg[:, :128])))
 
     def to_home(f):
         for hh in range(2):
@@ -357,7 +396,7 @@
     dad = total(field[0] * img[0])
 
     transform_t(img.at[0], tmp)
-    transform_l(tmp, fsend.at[1], T_FWD, fill=dad)
+    cosines_forward(tmp, fsend.at[1], fill=dad)
     cell_rows = pair_rows(cell)
     everyone(lambda c, m: remote(fsend.at[1, pair_rows(c * 2 + m)], frecv.at[1, cell_rows], 2, (c, m)))
     local(fsend.at[1, pair_rows(me)], frecv.at[1, cell_rows], 2)
@@ -392,18 +431,8 @@
     both_steps = alpha0 + alpha1 * beta
     for f in range(4):
         landed(out_recv.at[f], 10 + f)
-    out_recv[0] = both_steps * out_recv[0] + alpha1 * out_recv[2]
-    out_recv[1] = xp[...] - both_steps * out_recv[1] - alpha1 * out_recv[3]
-
-    def store_row(r, carry):
-        for e in range(2):
-            for lh in range(2):
-                row = pl.ds(lh * 64 + e * 32 + r, 1)
-                ox_ref[r, e : e + 1, lh * 512 : (lh + 1) * 512] = out_recv[0, row, :]
-                or_ref[r, e : e + 1, lh * 512 : (lh + 1) * 512] = out_recv[1, row, :]
-        return carry
-
-    lax.fori_loop(0, 30, store_row, 0)
+    y_ref[0] = both_steps * out_recv[0] + alpha1 * out_recv[2]
+    y_ref[1] = xp[...] - both_steps * out_recv[1] - alpha1 * out_recv[3]
 
     for n in range(2):
         sent(fsend.at[n, pl.ds(0, 510)], 2 * n)
@@ -425,12 +454,22 @@
             sent(out_send.at[f], 10 + f)
 
 
+def unpack(y_ref, *out_refs):
+    for n, out_ref in enumerate(out_refs):
+        for e in range(2):
+            for lh in range(2):
+                at = lh * 64 + e * 32
+                out_ref[:, e, lh * 512 : (lh + 1) * 512] = y_ref[n, at : at + 30, :]
+
+
 def on_device(right_side, stiffness, pairing, coupling):
     consts = [jnp.asarray(v) for v in tables()]
     shape = jax.ShapeDtypeStruct((30, 2, 1024), jnp.float32)
     vmem = pl.BlockSpec(memory_space=pltpu.VMEM)
     f32 = jnp.float32
-    scratch = [
+    far = pl.BlockSpec(memory_space=pltpu.HBM)
+    operands = (right_side.reshape(30, 2, 1024), stiffness, pairing, coupling, *consts)
+    scratch = [pltpu.VMEM(v.shape, v.dtype) for v in operands] + [
         pltpu.VMEM((128, 512), f32),
         pltpu.VMEM((128, 512), f32),
         pltpu.VMEM((2, 8, 512), f32),
@@ -450,7 +489,9 @@
         pltpu.VMEM(FIELD, f32),
         pltpu.VMEM(FIELD, f32),
         pltpu.VMEM((2,) + FIELD, f32),
-        pltpu.VMEM((384, 128), f32),
+        pltpu.VMEM((512, 384), jnp.bfloat16),
+        pltpu.VMEM((512, 384), jnp.bfloat16),
+        pltpu.VMEM((384, 256), jnp.bfloat16),
         pltpu.VMEM((256, 256), f32),
         pltpu.VMEM((256, 256), f32),
         pltpu.VMEM(FIELD, f32),
@@ -459,17 +500,19 @@
         pltpu.VMEM((3, 512, 512), f32),
         pltpu.SemaphoreType.DMA((14,)),
         pltpu.SemaphoreType.DMA((14,)),
+        pltpu.SemaphoreType.DMA((11,)),
     ]
-    x, r = pl.pallas_call(
+    packed = pl.pallas_call(
         kernel,
-        out_shape=(shape, shape),
-        in_specs=[vmem] * 11,
-        out_specs=(vmem, vmem),
+        out_shape=jax.ShapeDtypeStruct((2, 128, 512), f32),
+        in_specs=[far] * 11,
+        out_specs=vmem,
         scratch_shapes=scratch,
         compiler_params=pltpu.CompilerParams(
-            collective_id=0, has_side_effects=True, vmem_limit_bytes=44 * 1024 * 1024
+            collective_id=0, has_side_effects=True, vmem_limit_bytes=60 * 1024 * 1024
         ),
-    )(right_side.reshape(30, 2, 1024), stiffness, pairing, coupling, *consts)
+    )(*operands)
+    x, r = pl.pallas_call(unpack, out_shape=(shape, shape), in_specs=[vmem], out_specs=(vmem, vmem))(packed)
     return x.reshape(right_side.shape), r.reshape(right_side.shape)
 
 

time: 90 us -> 78.6 us (0.87)
  local copies, waits for them, and re-layouts: 10.6 us -> 0 us
    unnamed x24 -> x0, local copies, waits for them, and re-layouts: 10.6 us -> none
    pallas_call x1 -> x2, Pallas kernels: 78.3 us -> 77.9 us  [the longest x1 76 us: on_device(): pl.pallas_call(kernel, out_shape=jax.ShapeDtypeStruct((2, 128, 512), f32)...]
where the time goes in v2:
time: 78.6 us; the launch traced here: 78.5 us
  Pallas kernels  77.9 us (99%)
    pallas_call x1, Pallas kernels, on_device(): pl.pallas_call(kernel, out_shape=jax.ShapeDtypeStruct((2, 128, 512), f32)...  76 us
    pallas_call x1, Pallas kernels, on_device(): pl.pallas_call(unpack, out_shape=(shape, shape), in_specs=[vmem], out_spe...  1.87 us

profile of v2, /device:TPU:1, one launch (start us, length us, event | category | flops | bytes accessed | tf_op | source)
XLA Modules:
  0.0 78.5 jit_solution(8016433837043746666)
XLA Ops:
  0.6 76.0 %shard_map.122.y_ref = f32[2,128,512]{2,1,0:T(8,128)} custom-call(f32[30,2,1024]{2,1,0:T(2,128)} %bitcast.3, f32[4,2,1024]{2,1,0:T(2,128)} %st_far.1, s32[3,20]{1,0:T(4,128)} %pair_far.1, f32[3,20]{1,0:T(4,128)} %coup_far.1, f32[256,256]{1,0:T(8,128)} %constant.14.clone.h_far, f32[256,256]{1,0:T(8,128)} %constant.15.clone.both_far, ...), custom_call_target="tpu_custom_call" | custom-call | tf_op jit(solution)/shard_map/pallas_call | solution.py:505
  76.7 1.9 %shard_map.123 = (f32[30,2,1024]{2,1,0:T(2,128)}, f32[30,2,1024]{2,1,0:T(2,128)}) custom-call(f32[2,128,512]{2,1,0:T(8,128)} %shard_map.122.y_ref), custom_call_target="tpu_custom_call" | custom-call | tf_op jit(solution)/shard_map/pallas_call | solution.py:515

commit v3 on v2

--- a/solution.py
+++ b/solution.py
@@ -105,22 +105,24 @@
     gamma_lane = lane == GAMMA
     valid = lax.rem(lane, 32) < 30
 
+    z_parts = [lax.rem(z + zo, 8) * 8 for zo in Z_ORDER]
+
     def everyone(act):
-        z_parts = [lax.rem(z + zo, 8) * 8 for zo in Z_ORDER]
-        for yo in (2, 1, 3, 0):
-            y_part = lax.rem(y + yo, 4) * 2
+        def along(base, side, there, parts):
+            its_me, its_cell = base * 2 + there, base * 2 - side + there * 2
+            for part in parts:
+                act(base + part, there, its_me + 2 * part, its_cell + 2 * part)
+
+        for flip in ((0, 1, 1), (0, 1, 0), (1, 1, 1), (1, 1, 0), (1, 0, 1), (1, 0, 0), (0, 0, 1), (0, 0, 0)):
+            far_x, there, side = [1 - v if f else v for f, v in zip(flip, (xl, mode, core))]
+            line = far_x * 64 + side
 
             def step(i, carry):
-                k = 7 - i
-                base = lax.rem(xl + k // 4, 2) * 64 + y_part + lax.rem(core + lax.rem(k // 2, 2), 2)
-                there = lax.rem(mode + lax.rem(k, 2), 2)
-                for part in z_parts:
-                    act(base + part, there)
+                along(line + lax.rem(y + 1 + i, 4) * 2, side, there, z_parts)
                 return carry
 
-            lax.fori_loop(0, 8 if yo else 7, step, 0)
-        for part in z_parts[:-1]:
-            act(xl * 64 + y * 2 + core + part, mode)
+            lax.fori_loop(0, 4 if any(flip) else 3, step, 0)
+        along(xl * 64 + y * 2 + core, core, mode, z_parts[:-1])
 
     def remote(src, dst, sem, where):
         pltpu.make_async_remote_copy(
@@ -140,20 +142,17 @@
         return pl.ds(pl.multiple_of(index * 2, 2), 2)
 
     barrier = pltpu.get_barrier_semaphore()
-    everyone(lambda c, m: pl.semaphore_signal(barrier, 1, device_id=(c, m), device_id_type=MESH))
+    everyone(lambda c, m, d, n: pl.semaphore_signal(barrier, 1, device_id=(c, m), device_id_type=MESH))
 
     fetches[0].wait()
     fetches[1].wait()
     for part in range(4):
         xp[part * 32 + 24 : part * 32 + 32, :] = jnp.zeros((8, 512), jnp.float32)
 
-    def load_row(r, carry):
-        for e in range(2):
-            for lh in range(2):
-                xp[pl.ds(lh * 64 + e * 32 + r, 1), :] = x_ref[r, e : e + 1, lh * 512 : (lh + 1) * 512]
-        return carry
-
-    lax.fori_loop(0, 30, load_row, 0)
+    for e in range(2):
+        for lh in range(2):
+            at = lh * 64 + e * 32
+            xp[at : at + 30, :] = x_ref[:, e, lh * 512 : (lh + 1) * 512]
     for k in range(4):
         for e in range(2):
             for lh in range(2):
@@ -211,7 +210,7 @@
     pl.semaphore_wait(barrier, 255)
 
     my_rows = pair_rows(mode * 128 + circ)
-    everyone(lambda c, m: remote(fsend.at[0, pair_rows(c * 2 + m)], frecv.at[0, my_rows], 0, (c, m)))
+    everyone(lambda c, m, d, n: remote(fsend.at[0, pair_rows(d)], frecv.at[0, my_rows], 0, (c, m)))
     local(fsend.at[0, pair_rows(me)], frecv.at[0, my_rows], 0)
 
     sibling = (chip * 2 + 1 - core, mode)
@@ -266,11 +265,9 @@
             rsend[carried, pl.ds(r, 256, stride=2), :] = cells[:, r * 128 : (r + 1) * 128]
         mine = pair_rows(me)
 
-        def act(c, m):
-            there = 4 * (c // 2) + 2 * m + lax.rem(c, 2)
-            remote(rsend.at[carried, pair_rows(there)], rrecv.at[carried, mine], sem, (c, m))
-
-        everyone(act)
+        everyone(
+            lambda c, m, d, n: remote(rsend.at[carried, pair_rows(n)], rrecv.at[carried, mine], sem, (c, m))
+        )
         local(rsend.at[carried, pair_rows(cell)], rrecv.at[carried, mine], sem)
 
     landed(frecv.at[0], 0)
@@ -325,8 +322,9 @@
         cosines_back(rrecv.at[n], tmp)
         out = sines(tmp)
         for s in range(2):
-            field[n, s * 256 : (s + 1) * 256, :] = jnp.where(valid, out[:, s * 128 : (s + 1) * 128], 0.0)
-        remote(field.at[n], zsib.at[n], 5 + n, sibling)
+            part = pl.ds(s * 256, 256)
+            field[n, part, :] = jnp.where(valid, out[:, s * 128 : (s + 1) * 128], 0.0)
+            remote(field.at[n, part], zsib.at[n, part], (5 if s == 0 else 14) + n, sibling)
         return carried
 
     def operator(n):
@@ -357,7 +355,6 @@
             return carry
 
         lax.fori_loop(0, 8, inner, 0, unroll=True)
-        landed(zsib.at[n], 5 + n)
 
         def outer(g, carry):
             here = pl.ds(pl.multiple_of(g * 64, 64), 64)
@@ -372,7 +369,9 @@
                 t_low[here, at] = (acc - high.astype(jnp.float32)).astype(jnp.bfloat16)
             return carry
 
-        lax.fori_loop(0, 8, outer, 0, unroll=True)
+        for s in range(2):
+            landed(zsib.at[n, pl.ds(s * 256, 256)], (5 if s == 0 else 14) + n)
+            lax.fori_loop(4 * s, 4 * s + 4, outer, 0, unroll=True)
         large = dot16(t_high[...], gg[...])
         img[n] = t0[...] + (large[:, :128] + (large[:, 128:] + dot16(t_low[...], gg[:, :128])))
 
@@ -398,7 +397,7 @@
     transform_t(img.at[0], tmp)
     cosines_forward(tmp, fsend.at[1], fill=dad)
     cell_rows = pair_rows(cell)
-    everyone(lambda c, m: remote(fsend.at[1, pair_rows(c * 2 + m)], frecv.at[1, cell_rows], 2, (c, m)))
+    everyone(lambda c, m, d, n: remote(fsend.at[1, pair_rows(d)], frecv.at[1, cell_rows], 2, (c, m)))
     local(fsend.at[1, pair_rows(me)], frecv.at[1, cell_rows], 2)
     out_send[0] = jnp.transpose(field[0])
     to_home(0)
@@ -421,7 +420,7 @@
     dad = total((field[1] + beta * field[0]) * (img[1] + beta * img[0]))
     sum_out[...] = jnp.broadcast_to(dad, (8, 128))
     sum_in[pl.ds(me, 1), :] = jnp.broadcast_to(dad, (1, 128))
-    everyone(lambda c, m: remote(sum_out.at[pl.ds(0, 1)], sum_in.at[pl.ds(me, 1)], 4, (c, m)))
+    everyone(lambda c, m, d, n: remote(sum_out.at[pl.ds(0, 1)], sum_in.at[pl.ds(me, 1)], 4, (c, m)))
     out_send[2] = jnp.transpose(field[1])
     to_home(2)
     out_send[3] = jnp.transpose(img[1])
@@ -437,7 +436,8 @@
     for n in range(2):
         sent(fsend.at[n, pl.ds(0, 510)], 2 * n)
         sent(rsend.at[n, pl.ds(0, 510)], 1 + 2 * n)
-        sent(field.at[n], 5 + n)
+        sent(field.at[n, pl.ds(0, 256)], 5 + n)
+        sent(field.at[n, pl.ds(256, 256)], 14 + n)
     sent(sum_in.at[pl.ds(0, 255)], 4)
     sent(a_all.at[pl.ds(0, 4)], 9)
 
@@ -498,8 +498,8 @@
         pltpu.VMEM((4, 128, 512), f32),
         pltpu.VMEM((4, 128, 512), f32),
         pltpu.VMEM((3, 512, 512), f32),
-        pltpu.SemaphoreType.DMA((14,)),
-        pltpu.SemaphoreType.DMA((14,)),
+        pltpu.SemaphoreType.DMA((16,)),
+        pltpu.SemaphoreType.DMA((16,)),
         pltpu.SemaphoreType.DMA((11,)),
     ]
     packed = pl.pallas_call(

time: 78.6 us -> 78.3 us (level)
  no operation moved by 1% of the time
where the time goes in v3:
time: 78.3 us; the launch traced here: 78.2 us
  Pallas kernels  77.5 us (99%)
    pallas_call x1, Pallas kernels, on_device(): pl.pallas_call(kernel, out_shape=jax.ShapeDtypeStruct((2, 128, 512), f32)...  75.7 us
    pallas_call x1, Pallas kernels, on_device(): pl.pallas_call(unpack, out_shape=(shape, shape), in_specs=[vmem], out_spe...  1.87 us

profile of v3, /device:TPU:1, one launch (start us, length us, event | category | flops | bytes accessed | tf_op | source)
XLA Modules:
  0.0 78.2 jit_solution(7808359439416906552)
XLA Ops:
  0.6 75.7 %shard_map.122.y_ref = f32[2,128,512]{2,1,0:T(8,128)} custom-call(f32[30,2,1024]{2,1,0:T(2,128)} %bitcast.3, f32[4,2,1024]{2,1,0:T(2,128)} %st_far.1, s32[3,20]{1,0:T(4,128)} %pair_far.1, f32[3,20]{1,0:T(4,128)} %coup_far.1, f32[256,256]{1,0:T(8,128)} %constant.14.clone.h_far, f32[256,256]{1,0:T(8,128)} %constant.15.clone.both_far, ...), custom_call_target="tpu_custom_call" | custom-call | tf_op jit(solution)/shard_map/pallas_call | solution.py:505
  76.3 1.9 %shard_map.123 = (f32[30,2,1024]{2,1,0:T(2,128)}, f32[30,2,1024]{2,1,0:T(2,128)}) custom-call(f32[2,128,512]{2,1,0:T(8,128)} %shard_map.122.y_ref), custom_call_target="tpu_custom_call" | custom-call | tf_op jit(solution)/shard_map/pallas_call | solution.py:515

commit v4 on v3

--- a/solution.py
+++ b/solution.py
@@ -416,13 +416,13 @@
 
     rz1 = smoothed(1)
     beta = rz1 / rz0
+    out_send[2] = jnp.transpose(field[1])
+    to_home(2)
     operator(1)
     dad = total((field[1] + beta * field[0]) * (img[1] + beta * img[0]))
     sum_out[...] = jnp.broadcast_to(dad, (8, 128))
     sum_in[pl.ds(me, 1), :] = jnp.broadcast_to(dad, (1, 128))
     everyone(lambda c, m, d, n: remote(sum_out.at[pl.ds(0, 1)], sum_in.at[pl.ds(me, 1)], 4, (c, m)))
-    out_send[2] = jnp.transpose(field[1])
-    to_home(2)
     out_send[3] = jnp.transpose(img[1])
     to_home(3)
     landed(sum_in.at[pl.ds(0, 255)], 4)

time: 78.3 us -> 75.5 us (0.964)
  Pallas kernels: 77.5 us -> 74.7 us
    pallas_call x1, Pallas kernels: 75.7 us -> 72.9 us  [on_device(): pl.pallas_call(kernel, out_shape=jax.ShapeDtypeStruct((2, 128, 512), f32)...]
where the time goes in v4:
time: 75.5 us; the launch traced here: 75.4 us
  Pallas kernels  74.7 us (99%)
    pallas_call x1, Pallas kernels, on_device(): pl.pallas_call(kernel, out_shape=jax.ShapeDtypeStruct((2, 128, 512), f32)...  72.9 us
    pallas_call x1, Pallas kernels, on_device(): pl.pallas_call(unpack, out_shape=(shape, shape), in_specs=[vmem], out_spe...  1.87 us

profile of v4, /device:TPU:1, one launch (start us, length us, event | category | flops | bytes accessed | tf_op | source)
XLA Modules:
  0.0 75.4 jit_solution(15215450942054364457)
XLA Ops:
  0.6 72.9 %shard_map.122.y_ref = f32[2,128,512]{2,1,0:T(8,128)} custom-call(f32[30,2,1024]{2,1,0:T(2,128)} %bitcast.3, f32[4,2,1024]{2,1,0:T(2,128)} %st_far.1, s32[3,20]{1,0:T(4,128)} %pair_far.1, f32[3,20]{1,0:T(4,128)} %coup_far.1, f32[256,256]{1,0:T(8,128)} %constant.14.clone.h_far, f32[256,256]{1,0:T(8,128)} %constant.15.clone.both_far, ...), custom_call_target="tpu_custom_call" | custom-call | tf_op jit(solution)/shard_map/pallas_call | solution.py:505
  73.5 1.9 %shard_map.123 = (f32[30,2,1024]{2,1,0:T(2,128)}, f32[30,2,1024]{2,1,0:T(2,128)}) custom-call(f32[2,128,512]{2,1,0:T(8,128)} %shard_map.122.y_ref), custom_call_target="tpu_custom_call" | custom-call | tf_op jit(solution)/shard_map/pallas_call | solution.py:515
